TPU v7x, 32 devices: a whole 2x2x4 slice. The times are simulated.
32 devices in a mesh: group: 2 (over x), tm: 2 (over core), space: 8 (over z, y).
Axes of the slice: x: 2, y: 2, z: 4, core: 2. Of those that a mesh axis runs over, the one named last changes fastest.
Arguments:
- start_old: float32 [4, 3, 1024, 1024], P(('group', 'tm'), None, 'space'), parts along dimension 0, may hold values from -3 to 3
- incoming: float32 [6, 512, 512], P('group', 'space'), parts along dimension 0, may hold values from -3 to 3
Outputs:
- new_states: float32 [4, 3, 1024, 1024], P(('group', 'tm'), None, 'space'), parts along dimension 0
There are 2 independent parts, one for each index of `group`. A program takes and returns all parts, laid end to end along the dimension named above; each array names one. Nothing has to cross between parts.
All inputs are finite; a program needn't handle non-finite values.
Results may differ from a plain program's by a relative error of at most 0.0001.
Values sent between devices are 32-bit elements; how exact they have to be, the bound alone decides.
A program may use at most 192 MiB of HBM per device.

v0:
```python
import functools
import math

import jax
import jax.numpy as jnp
import numpy as np
from jax import lax
from jax.experimental import pallas as pl
from jax.experimental.pallas import tpu as pltpu
from jax.sharding import PartitionSpec as P

RATIO = 2
STEPS = 2
TIME_STEP = 0.25
CORIOLIS = 0.5
HALO = 8
CORES = 2
MESH = pl.DeviceIdType.MESH


def halves(table):
    high = table.astype(jnp.bfloat16)
    return high, (table - high.astype(np.float32)).astype(jnp.bfloat16)


def split(a):
    high = a.astype(jnp.bfloat16)
    return high, (a - high.astype(jnp.float32)).astype(jnp.bfloat16)


def dot(a, b, sides=(1, 0)):
    dims = (((sides[0],), (sides[1],)), ((), ()))
    return lax.dot_general(a, b, dims, preferred_element_type=jnp.float32)


def tables(nc, parts):
    half, rows = nc // 2, nc // parts
    x = np.arange(nc)
    angle = 2.0 * math.pi / nc * (np.outer(np.arange(half), x) % nc)
    real, imag = np.cos(angle), -np.sin(angle)
    imag[0] = (-1.0) ** x
    forward = np.stack([real, imag])
    wide = 0.5 * np.repeat(forward, RATIO, axis=2)

    angle = 2.0 * math.pi / nc * (np.outer(x, x) % nc)
    cos, sin = np.cos(angle), np.sin(angle)
    along = np.stack([np.stack([cos, -sin], 1), np.stack([sin, cos], 1)])
    back = np.stack([np.stack([cos, sin], 1), np.stack([-sin, cos], 1)])
    along = along.reshape(2, parts, rows, 2 * nc).transpose(1, 0, 2, 3).reshape(2 * nc, 2 * nc)
    back = back.reshape(2 * nc, 2, parts, rows).transpose(0, 2, 1, 3).reshape(2 * nc, 2 * nc)

    scale = np.full((1, half, 1), 2.0 / (nc * nc))
    scale[:, 0] = 1.0 / (nc * nc)
    inverse = np.repeat(forward * scale, RATIO, axis=2).reshape(nc, -1)

    index = np.where(x < half, x, x - nc)
    index = np.where(x == half, 0, index)
    wave = index * (2.0 * math.pi / (nc * RATIO))
    omega = np.sqrt(CORIOLIS**2 + wave[:half, None] ** 2 + wave[None, :] ** 2)
    duration = STEPS * TIME_STEP
    sine = np.sin(omega * duration) / omega
    versine = (1.0 - np.cos(omega * duration)) / omega**2
    single = lambda a: np.asarray(a, np.float32)
    return [single(a) for a in (forward, wide, along, back, inverse, wave, sine, versine)]


def tendency(window):
    width = window[0].shape[-1]
    mid = [a[8:16] for a in window]
    south = [a[7:15] for a in window]
    north = [a[9:17] for a in window]
    west = [pltpu.roll(a, 1, 1) for a in mid]
    east = [pltpu.roll(a, width - 1, 1) for a in mid]
    _, u, v = mid
    flux = (1.0 + east[0]) * east[1] - (1.0 + west[0]) * west[1]
    flux = flux + ((1.0 + north[0]) * north[2] - (1.0 + south[0]) * south[2])
    half_u, half_v = 0.5 * u, 0.5 * v
    rate_u = CORIOLIS * v - (
        half_u * (east[1] - west[1]) + half_v * (north[1] - south[1]) + 0.5 * (east[0] - west[0])
    )
    rate_v = -(CORIOLIS * u) - (
        half_u * (east[2] - west[2]) + half_v * (north[2] - south[2]) + 0.5 * (north[0] - south[0])
    )
    return mid, (-0.5 * flux, rate_u, rate_v)


def rows_at(row):
    return row if isinstance(row, int) else pl.multiple_of(row, 8)


def heun(rows, width, now, first):
    blocks = (rows + 2 * HALO) // 8
    pad = jnp.zeros((HALO, width), jnp.float32)

    def clear():
        for f in range(3):
            for ref in (now, first):
                ref[f, 0:8] = pad
                ref[f, 24 + rows : 32 + rows] = pad

    def window(ref, block):
        at = rows_at(block * 8)
        return [ref[f, pl.ds(at, 24)] for f in range(3)]

    def predict(block, _):
        mid, rate = tendency(window(now, block))
        at = rows_at(block * 8 + 8)
        for f in range(3):
            first[f, pl.ds(at, 8)] = mid[f] + TIME_STEP * rate[f]
        return 0

    def correct(out, shift):
        def body(block, _):
            mid, rate = tendency(window(first, block))
            at = rows_at(block * 8 + 8)
            to = rows_at(block * 8 + 8 - shift)
            for f in range(3):
                out[f, pl.ds(to, 8)] = 0.5 * (now[f, pl.ds(at, 8)] + mid[f] + TIME_STEP * rate[f])
            return 0

        return body

    def inner():
        clear()
        lax.fori_loop(2, blocks - 2, predict, 0)

    def edges():
        for block in (0, 1, blocks - 2, blocks - 1):
            predict(block, 0)
        lax.fori_loop(0, blocks, correct(now, 0), 0)

    def last(fine):
        lax.fori_loop(0, blocks, predict, 0)
        lax.fori_loop(1, blocks - 1, correct(fine, 16), 0)

    return inner, edges, last


def apply_operator(s, a, b):
    (hr, hi), (ur, ui), (vr, vi) = s
    return (
        (a * ui + b * vi, -(a * ur + b * vr)),
        (a * hi + CORIOLIS * vr, CORIOLIS * vi - a * hr),
        (b * hi - CORIOLIS * ur, -(b * hr) - CORIOLIS * ui),
    )


def kernel(
    size, state, incoming_far, pairs_far, twice_far, north_far,
    wide_h_far, wide_l_far, short_h_far, short_l_far, along_h, along_l, back_h, back_l, inverse_h, inverse_l,
    east_far, sine_far, versine_far, out,
    incoming, pairs, twice, north, now, first, fine, gap, mine, theirs, landed, arrived, acc, kept, relayed, change,
    leaving, going, returned, east, sine, versine,
    wide_h, wide_l, short_h, short_l, ah, al, bh, bl, ih, il,
    fetch, store, rim_send, rim_recv, t_send, t_recv, d_send, d_recv, e_send, e_recv, g_send, g_recv, h_send, h_recv,
):
    fields, rows, nc = incoming_far.shape
    wide_rows, width = state.shape[1:]
    half = nc // 2
    count = half // size
    each = count // CORES
    me, slot = lax.axis_index("space"), lax.axis_index("tm")
    peers = [lax.rem(me + d, size) for d in range(size)]
    origins = [lax.rem(me + size - d, size) for d in range(size)]

    share = pl.ds(pl.multiple_of(me * count, count), count)
    fetches = [
        pltpu.make_async_copy(source, target, fetch.at[n])
        for n, (source, target) in enumerate(
            (
                (state, now.at[:, pl.ds(16, wide_rows)]),
                (pairs_far, pairs),
                (wide_h_far, wide_h),
                (wide_l_far, wide_l),
                (incoming_far, incoming),
                (short_h_far, short_h),
                (short_l_far, short_l),
                (along_h, ah),
                (along_l, al),
                (east_far.at[share], east),
                (sine_far.at[share], sine),
                (versine_far.at[share], versine),
                (north_far, north),
                (back_h, bh),
                (back_l, bl),
                (twice_far, twice),
                (inverse_h, ih),
                (inverse_l, il),
            )
        )
    ]
    barrier = pltpu.get_barrier_semaphore()
    for d, peer in enumerate(peers):
        for core in range(CORES):
            if d > 0:
                pl.semaphore_signal(barrier, inc=1, device_id={"space": peer, "tm": core}, device_id_type=MESH)
    pl.semaphore_signal(barrier, inc=1, device_id={"tm": 1 - slot}, device_id_type=MESH)
    for copy in fetches:
        copy.start()

    def send(source, target, sender, receiver, peer, core):
        return pltpu.make_async_remote_copy(
            src_ref=source, dst_ref=target, send_sem=sender, recv_sem=receiver,
            device_id={"space": peer, "tm": core}, device_id_type=MESH,
        )

    rims = [
        send(
            state.at[:, pl.ds(source, HALO)], now.at[:, pl.ds(target, HALO)],
            rim_send.at[n], rim_recv.at[n], peer, slot,
        )
        for n, (source, target, peer) in enumerate(
            ((wide_rows - HALO, 8, peers[1]), (0, 16 + wide_rows, peers[-1]))
        )
    ]
    early = [send(gap.at[p], landed.at[me], d_send.at[n], d_recv.at[n], p, 1) for n, p in enumerate(peers)]
    ahead = send(gap, theirs, t_send.at[0], t_recv.at[0], me, 0)
    relay = send(kept.at[0], relayed, t_send.at[1], t_recv.at[1], me, 0)
    back = [send(leaving.at[p], returned.at[me], e_send.at[n], e_recv.at[n], p, 0) for n, p in enumerate(peers)]
    late = [
        [send(mine.at[p, c], arrived.at[me], g_send.at[n, c], g_recv.at[n], p, c) for c in range(CORES)]
        for n, p in enumerate(peers)
    ]
    home = [
        send(going.at[p], returned.at[me, slot], h_send.at[n], h_recv.at[n, slot], p, 1)
        for n, p in enumerate(peers)
    ]
    homes = [
        [send(going.at[p], returned.at[me, c], h_send.at[n], h_recv.at[n, c], p, 1) for c in range(CORES)]
        for n, p in enumerate(peers)
    ]

    def spectra_of(stacked, high, low):
        up, down = split(stacked)
        return dot(high, up, (1, 1)) + (dot(high, down, (1, 1)) + dot(low, up, (1, 1)))

    def x_spectra(ref):
        parts = [split(ref[f]) for f in range(fields)]
        averaged = [dot(pairs[...], up) + dot(pairs[...], down) for up, down in parts]
        return spectra_of(jnp.concatenate(averaged, 0), wide_h[...], wide_l[...])

    def lay_out(value, put):
        for f in range(fields):
            both = value[:, f * rows : (f + 1) * rows]
            both = jnp.concatenate([both[:half], both[half:]], 1)
            for j in range(size):
                for c in range(CORES):
                    at = (j * CORES + c) * each
                    put((j, c, f), both[at : at + each])

    pl.semaphore_wait(barrier, CORES * size - 1)
    for copy in rims:
        copy.start()

    for copy in fetches[:4]:
        copy.wait()

    def put_gap(at, value):
        gap[at] = -value

    def add_gap(at, value):
        gap[at] += value

    def put_mine(at, value):
        mine[at] = theirs[at] + value

    lay_out(x_spectra(now.at[:, pl.ds(16, wide_rows)]), put_gap)
    for copy in fetches[4:7]:
        copy.wait()

    @pl.when(slot == 0)
    def _():
        fresh = jnp.concatenate([incoming[f] for f in range(fields)], 0)
        lay_out(spectra_of(fresh, short_h[...], short_l[...]), add_gap)
        for copy in early:
            copy.start()

    @pl.when(slot == 1)
    def _():
        ahead.start()

    inner, edges, last = heun(wide_rows, width, now, first)
    inner()
    for copy in rims:
        copy.wait()
    edges()

    def y_spectra(blocks):
        up, down = split(jnp.concatenate(blocks, 1))
        return dot(up, ah[...]) + (dot(down, ah[...]) + dot(up, al[...]))

    def y_fields(value):
        up, down = split(value)
        return dot(up, bh[...]) + (dot(down, bh[...]) + dot(up, bl[...]))

    def propagate(source, target, core):
        tile = min(each, 8)
        for r in range(0, each, tile):
            at = pl.ds(core * each + r, tile)
            wave = slice(r, r + tile)
            spectra = [(source[f, wave, :nc], source[f, wave, nc:]) for f in range(fields)]
            once = apply_operator(spectra, east[at], north[:tile])
            twofold = apply_operator(once, east[at], north[:tile])
            for f in range(fields):
                for part, lanes in enumerate((slice(0, nc), slice(nc, 2 * nc))):
                    target[f, wave, lanes] = (
                        spectra[f][part] + sine[at] * once[f][part] + versine[at] * twofold[f][part]
                    )

    for copy in fetches[7:]:
        copy.wait()

    @pl.when(slot == 1)
    def _():
        for copy in early:
            copy.wait_recv()
        order = [(c, f) for c in range(CORES) for f in range(fields)]
        value = y_spectra(
            [jnp.concatenate([landed[j, c, f] for c, f in order], 0) for j in range(size)]
        )
        for n, (c, f) in enumerate(order):
            acc[c, f] = value[n * each : (n + 1) * each]
        for c in range(CORES):
            propagate(acc.at[c], kept.at[c], c)
        relay.start()
        value = y_fields(jnp.concatenate([kept[c, f] for c, f in order], 0))
        for j in range(size):
            for n, (c, f) in enumerate(order):
                leaving[j, c, f] = value[n * each : (n + 1) * each, j * 2 * rows : (j + 1) * 2 * rows]
        for copy in back:
            copy.start()

    last(fine)

    @pl.when(slot == 0)
    def _():
        for copy in early:
            copy.wait_send()
        ahead.wait_recv()
        lay_out(x_spectra(fine), put_mine)
        for n in range(size):
            for c in range(CORES):
                if n > 0 or c > 0:
                    late[n][c].start()
        arrived[me] = mine[me, 0]
        relay.wait_recv()

    @pl.when(slot == 1)
    def _():
        relay.wait_send()
        relayed[...] = kept[1]
        late[0][1].wait_recv()

    for n in range(1, size):
        late[n][0].wait_recv()
    value = y_spectra([jnp.concatenate([arrived[j, f] for f in range(fields)], 0) for j in range(size)])
    for f in range(fields):
        acc[0, f] = value[f * each : (f + 1) * each] + relayed[f]

    propagate_at(propagate, acc, change, slot)
    value = y_fields(jnp.concatenate([change[f] for f in range(fields)], 0))
    for j in range(size):
        for f in range(fields):
            going[j, f] = value[f * each : (f + 1) * each, j * 2 * rows : (j + 1) * 2 * rows]
    for copy in home[1:]:
        copy.start()

    @pl.when(slot == 0)
    def _():
        home[0].start()
        for n in range(size):
            for c in range(CORES):
                if n > 0 or c > 0:
                    late[n][c].wait_send()
        for copy in back:
            copy.wait_recv()

    @pl.when(slot == 1)
    def _():
        returned[me, 1] = going[me]
        ahead.wait_send()
        for copy in back:
            copy.wait_send()
        homes[0][0].wait_recv()
        for n in range(1, size):
            for c in range(CORES):
                homes[n][c].wait_recv()

    stores = []
    for f in range(fields):
        spectrum = jnp.concatenate([returned[j, c, f] for j in range(size) for c in range(CORES)], 0)
        up, down = (
            jnp.concatenate([dot(twice[c], part, (1, 1)) for c in range(2)], 1).astype(jnp.bfloat16)
            for part in split(spectrum)
        )
        fine[f] += dot(up, ih[...]) + (dot(down, ih[...]) + dot(up, il[...]))
        stores.append(pltpu.make_async_copy(fine.at[f], out.at[f], store.at[f]))
        stores[-1].start()

    for copy in home[1:]:
        copy.wait_send()

    @pl.when(slot == 0)
    def _():
        home[0].wait_send()

    for copy in stores:
        copy.wait()


def propagate_at(propagate, acc, change, slot):
    for core in range(CORES):
        @pl.when(slot == core)
        def _():
            propagate(acc.at[0], change, core)


def shards(start_old, incoming):
    size = lax.axis_size("space")
    state = start_old[0]
    width = state.shape[2]
    fields, rows, nc = incoming.shape
    half = nc // 2
    count = half // size
    each = count // CORES
    forward, wide, along, back, inverse, wave, sine, versine = tables(nc, size)
    pairs = np.repeat(np.eye(rows, dtype=np.float32), RATIO, axis=1)
    twice = np.zeros((2, RATIO * rows, 2 * rows), np.float32)
    twice[0, :, :rows] = twice[1, :, rows:] = pairs.T

    flat = lambda table: halves(table.reshape(nc, -1))
    east = np.repeat(wave[:half, None], nc, axis=1)
    north = np.repeat(wave[None, :], 8, axis=0)
    operands = [state, incoming, (0.5 * pairs).astype(jnp.bfloat16), twice.astype(jnp.bfloat16), north]
    distant = [*flat(wide), *flat(forward), *halves(along), *halves(back), *halves(inverse)]
    padded = (fields, state.shape[1] + 4 * HALO, width)
    blocks = (size, CORES, fields, each, 2 * rows)
    single = (size, fields, each, 2 * rows)
    whole = (fields, each, 2 * nc)
    shapes = [north.shape, padded, padded, state.shape]
    shapes += [blocks] * 4 + [single] + [(CORES, *whole)] * 2 + [whole] * 2
    shapes += [blocks, single, blocks] + [(count, nc)] * 3
    buffers = [pltpu.VMEM(incoming.shape, jnp.float32)]
    buffers += [pltpu.VMEM(table.shape, jnp.bfloat16) for table in operands[2:4]]
    buffers += [pltpu.VMEM(shape, jnp.float32) for shape in shapes]
    far = pl.BlockSpec(memory_space=pltpu.HBM)
    inputs = len(operands) + len(distant) + 3
    dma = pltpu.SemaphoreType.DMA
    result = pl.pallas_call(
        functools.partial(kernel, size),
        out_shape=jax.ShapeDtypeStruct(state.shape, jnp.float32),
        in_specs=[far] * inputs,
        out_specs=far,
        scratch_shapes=buffers
        + [pltpu.VMEM(table.shape, jnp.bfloat16) for table in distant]
        + [dma((inputs,)), dma((fields,))]
        + [dma((2,))] * 4
        + [dma((size,))] * 4
        + [dma((size, CORES)), dma((size,)), dma((size,)), dma((size, CORES))],
        compiler_params=pltpu.CompilerParams(
            collective_id=0, has_side_effects=True, vmem_limit_bytes=(64 << 20) - (128 << 10)
        ),
        cost_estimate=pl.CostEstimate(
            flops=40 * fields * count * nc * nc, bytes_accessed=32 * nc * nc, transcendentals=0
        ),
    )(*operands, *distant, east, sine, versine)
    return result[None]


def solution(mesh):
    placed = (P(("group", "tm"), None, "space", None), P("group", "space", None))
    return jax.shard_map(
        shards,
        mesh=mesh,
        in_specs=placed,
        out_specs=P(("group", "tm"), None, "space", None),
        check_vma=False,
    )
```

profile of v0, /device:TPU:1, one launch (start us, length us, event | category | flops | bytes accessed | tf_op | source)
XLA Modules:
  0.0 41.9 jit_solution(15655952708093281196)
XLA Ops:
  0.0 39.2 %shard_map.172 = f32[3,128,1024]{2,1,0:T(8,128)} custom-call(f32[3,128,1024]{2,1,0:T(8,128)} %bitcast.3, f32[3,64,512]{2,1,0:T(8,128)} %incoming_far.1, bf16[64,128]{1,0:T(8,128)(2,1)} %constant.32.clone.pairs_far, bf16[2,128,128]{2,1,0:T(8,128)(2,1)} %constant.33.clone.twice_far, f32[8,512]{1,0:T(8,128)} %constant.34.clone.north_far, ...), custom_call_target="tpu_custom_call" | custom-call | flops 1006632960 | bytes 8388608 | tf_op jit(solution)/shard_map/pallas_call | solution.py:449
  39.2 2.7 %copy.20 = f32[1,3,128,1024]{3,2,1,0:T(8,128)} copy(f32[1,3,128,1024]{3,2,1,0:T(8,128)} %bitcast.2) | data formatting | bytes 3145728
where the time goes:
time: 42.1 us; the launch traced here: 41.9 us
  Pallas kernels  39.2 us (93%)
  local copies, waits for them, and re-layouts  2.73 us (6%)
    pallas_call x1, Pallas kernels, shards(): pl.pallas_call(functools.partial(kernel, size), out_shape=jax.ShapeDtypeS...  39.2 us
    unnamed x1, local copies, waits for them, and re-layouts  2.73 us

commit v1 on v0

v1 whole, which is shorter than its diff:
```python
import functools
import math

import jax
import jax.numpy as jnp
import numpy as np
from jax import lax
from jax.experimental import pallas as pl
from jax.experimental.pallas import tpu as pltpu
from jax.sharding import PartitionSpec as P

RATIO = 2
STEPS = 2
TIME_STEP = 0.25
CORIOLIS = 0.5
HALO = 8
RIM = 4
CORES = 2
LANES = 128
MESH = pl.DeviceIdType.MESH


def halves(table):
    high = table.astype(jnp.bfloat16)
    return high, (table - high.astype(np.float32)).astype(jnp.bfloat16)


def split(a):
    high = a.astype(jnp.bfloat16)
    return high, (a - high.astype(jnp.float32)).astype(jnp.bfloat16)


def dot(a, b, sides=(1, 0)):
    dims = (((sides[0],), (sides[1],)), ((), ()))
    return lax.dot_general(a, b, dims, preferred_element_type=jnp.float32)


def dot_split(a, high, low):
    up, down = split(a)
    count = a.shape[0]
    both = dot(jnp.concatenate([up, down], 0), high)
    return both[:count] + (both[count:] + dot(up, low))


def dot_table(high, low, a):
    up, down = split(a)
    count = a.shape[0]
    both = dot(high, jnp.concatenate([up, down], 0), (1, 1))
    return both[:, :count] + (both[:, count:] + dot(low, up, (1, 1)))


def tables(nc):
    half = nc // 2
    order = np.concatenate([np.arange(0, half, 2), np.arange(1, half, 2)])
    angle = 2.0 * math.pi / nc * (np.outer(order, np.arange(half)) % nc)
    real, imag = np.cos(angle), -np.sin(angle)
    imag[0] = (-1.0) ** np.arange(half)
    scale = np.full((half, 1), 2.0 / (nc * nc))
    scale[0] = 1.0 / (nc * nc)
    halved = lambda a: a.reshape(2, half // 2, half)
    forward = np.stack([halved(real), halved(imag)], 1).reshape(2, half, half)
    inverse = np.stack([halved(real * scale), halved(imag * scale)], 1).reshape(2, half, half)
    wide = np.repeat(forward / RATIO**2, RATIO, axis=2)
    inverse = np.repeat(inverse, RATIO, axis=2)

    y = np.arange(half)
    angle = 2.0 * math.pi / half * (np.outer(y, y) % half)
    turn = np.concatenate([np.cos(angle), np.sin(angle)], 1)
    angle = 2.0 * math.pi / nc * y
    twiddle = np.repeat(np.stack([np.cos(angle), -np.sin(angle)])[:, None], 8, axis=1)

    index = np.arange(nc)
    index = np.where(index < half, index, index - nc)
    index = np.where(index == -half, 0, index)
    wave = index * (2.0 * math.pi / (nc * RATIO))
    east = wave[order]
    north = np.concatenate([wave[0::2], wave[1::2]])
    omega = np.sqrt(CORIOLIS**2 + east[:, None] ** 2 + north[None, :] ** 2)
    duration = STEPS * TIME_STEP
    sine = np.sin(omega * duration) / omega
    versine = (1.0 - np.cos(omega * duration)) / omega**2
    single = lambda a: np.asarray(a, np.float32)
    return [single(a) for a in (forward, wide, turn, twiddle, inverse, east, north, sine, versine)]


def slopes(ref, at):
    blocks, lanes = ref.shape[1], ref.shape[3]
    lane = lax.broadcasted_iota(jnp.int32, (8, lanes), 1)
    begin, end = lane == 0, lane == lanes - 1
    mids = [[None] * blocks for _ in range(3)]
    rights = [[None] * blocks for _ in range(3)]
    lefts = [[None] * blocks for _ in range(3)]

    def mid(f, n):
        if mids[f][n] is None:
            mids[f][n] = ref[f, n, pl.ds(at, 8)]
        return mids[f][n]

    def right(f, n):
        if rights[f][n] is None:
            rights[f][n] = pltpu.roll(mid(f, n), 1, 1)
        return rights[f][n]

    def left(f, n):
        if lefts[f][n] is None:
            lefts[f][n] = pltpu.roll(mid(f, n), lanes - 1, 1)
        return lefts[f][n]

    for n in range(blocks):
        before, after = (n - 1) % blocks, (n + 1) % blocks
        hw, uw, vw = (jnp.where(begin, right(f, before), right(f, n)) for f in range(3))
        he, ue, ve = (jnp.where(end, left(f, after), left(f, n)) for f in range(3))
        hs, us, vs = (ref[f, n, pl.ds(at - 1, 8)] for f in range(3))
        hn, un, vn = (ref[f, n, pl.ds(at + 1, 8)] for f in range(3))
        h, u, v = (mid(f, n) for f in range(3))
        ux, vy = ue - uw, vn - vs
        rate_h = (ux + (he * ue - hw * uw)) + (vy + (hn * vn - hs * vs))
        rate_u = (u * ux + v * (un - us)) + ((he - hw) - v)
        rate_v = (u * (ve - vw) + v * vy) + ((hn - hs) + u)
        yield n, (h, u, v), (rate_h, rate_u, rate_v)


def heun(rows, now, first):
    blocks = (rows + 2 * HALO) // 8
    unit = 0.5 * TIME_STEP

    def rows_at(block):
        return block * 8 if isinstance(block, int) else pl.multiple_of(block * 8, 8)

    def predict(block, _):
        at = rows_at(block + 1)
        for n, mid, rate in slopes(now, at):
            for f in range(3):
                first[f, n, pl.ds(at, 8)] = mid[f] - unit * rate[f]
        return 0

    def correct(out, shift):
        def body(block, _):
            at, to = rows_at(block + 1), rows_at(block + 1 - shift)
            for n, mid, rate in slopes(first, at):
                for f in range(3):
                    out[f, n, pl.ds(to, 8)] = (
                        0.5 * (now[f, n, pl.ds(at, 8)] + mid[f]) - (0.5 * unit) * rate[f]
                    )
            return 0

        return body

    def inner():
        lax.fori_loop(2, blocks - 2, predict, 0)

    def edges():
        def edge(n, _):
            predict(jnp.where(n < 2, n, n + blocks - 4), 0)
            return 0

        lax.fori_loop(0, 4, edge, 0)
        lax.fori_loop(0, blocks, correct(now, 0), 0)

    def last(fine):
        lax.fori_loop(0, blocks, predict, 0)
        lax.fori_loop(1, blocks - 1, correct(fine, 2), 0)

    return inner, edges, last


def apply_operator(s, a, b):
    (hr, hi), (ur, ui), (vr, vi) = s
    return (
        (a * ui + b * vi, -(a * ur + b * vr)),
        (a * hi + CORIOLIS * vr, CORIOLIS * vi - a * hr),
        (b * hi - CORIOLIS * ur, -(b * hr) - CORIOLIS * ui),
    )


def kernel(
    size, state, incoming_far, mirror_far, north_far, twiddle_far,
    wide_h_far, wide_l_far, short_h_far, short_l_far, turn_h, turn_l, inverse_h, inverse_l,
    east_far, sine_far, versine_far, out,
    incoming, mirror, north, twiddle, rim_in, now, first, fine, gap, mine, theirs, landed, arrived, acc, kept, relayed, change,
    leaving, going, returned, east, sine, versine,
    wide_h, wide_l, short_h, short_l, th, tl, ih, il,
    fetch, store, rim_send, rim_recv, t_send, t_recv, d_send, d_recv, e_send, e_recv, g_send, g_recv, h_send, h_recv,
):
    fields, rows, nc = incoming_far.shape
    wide_rows, width = state.shape[1:]
    strips, lanes = now.shape[1], now.shape[3]
    half = nc // 2
    count = half // size
    each = count // CORES
    me, slot = lax.axis_index("space"), lax.axis_index("tm")
    peers = [lax.rem(me + d, size) for d in range(size)]
    origins = [lax.rem(me + size - d, size) for d in range(size)]

    share = pl.ds(pl.multiple_of(me * count, count), count)
    fetches = [
        pltpu.make_async_copy(source, target, fetch.at[n])
        for n, (source, target) in enumerate(
            (
                *(
                    (state.at[:, :, pl.ds(n * lanes, lanes)], now.at[:, n, pl.ds(2 * HALO, wide_rows)])
                    for n in range(strips)
                ),
                (wide_h_far, wide_h),
                (wide_l_far, wide_l),
                (incoming_far, incoming),
                (short_h_far, short_h),
                (short_l_far, short_l),
                (turn_h, th),
                (turn_l, tl),
                (twiddle_far, twiddle),
                (north_far, north),
                (east_far.at[share], east),
                (sine_far.at[share], sine),
                (versine_far.at[share], versine),
                (mirror_far, mirror),
                (inverse_h, ih),
                (inverse_l, il),
            )
        )
    ]
    rim_in[...] = jnp.zeros_like(rim_in)
    pad = jnp.zeros((fields, strips, HALO, lanes), jnp.float32)
    for ref in (now, first):
        ref[:, :, :HALO] = pad
        ref[:, :, 3 * HALO + wide_rows :] = pad

    barrier = pltpu.get_barrier_semaphore()
    for d, peer in enumerate(peers):
        for core in range(CORES):
            if d > 0:
                pl.semaphore_signal(barrier, inc=1, device_id={"space": peer, "tm": core}, device_id_type=MESH)
    pl.semaphore_signal(barrier, inc=1, device_id={"tm": 1 - slot}, device_id_type=MESH)
    for copy in fetches[: strips + 5]:
        copy.start()

    def send(source, target, sender, receiver, peer, core):
        return pltpu.make_async_remote_copy(
            src_ref=source, dst_ref=target, send_sem=sender, recv_sem=receiver,
            device_id={"space": peer, "tm": core}, device_id_type=MESH,
        )

    rims = [
        send(
            state.at[:, pl.ds(source, RIM)], rim_in.at[n, :, pl.ds(target, RIM)],
            rim_send.at[n], rim_recv.at[n], peer, slot,
        )
        for n, (source, target, peer) in enumerate(
            ((wide_rows - RIM, HALO - RIM, peers[1]), (0, 0, peers[-1]))
        )
    ]
    early = [send(gap.at[p], landed.at[me], d_send.at[n], d_recv.at[n], p, 1) for n, p in enumerate(peers)]
    ahead = send(gap, theirs, t_send.at[0], t_recv.at[0], me, 0)
    relay = send(kept.at[0], relayed, t_send.at[1], t_recv.at[1], me, 0)
    back = [send(leaving.at[p], returned.at[me], e_send.at[n], e_recv.at[n], p, 0) for n, p in enumerate(peers)]
    late = [
        [send(mine.at[p, c], arrived.at[me], g_send.at[n, c], g_recv.at[n], p, c) for c in range(CORES)]
        for n, p in enumerate(peers)
    ]
    home = [
        send(going.at[p], returned.at[me, slot], h_send.at[n], h_recv.at[n, slot], p, 1)
        for n, p in enumerate(peers)
    ]
    homes = [
        [send(going.at[p], returned.at[me, c], h_send.at[n], h_recv.at[n, c], p, 1) for c in range(CORES)]
        for n, p in enumerate(peers)
    ]

    def x_spectra(value, high, low, put):
        middle = value.shape[1] // 2
        west, east_side = value[:, :middle], value[:, middle:]
        for parity, part in enumerate((west + east_side, west - east_side)):
            found = dot_table(high[parity], low[parity], part)
            for f in range(fields):
                both = found[:, f * rows : (f + 1) * rows]
                both = jnp.concatenate([both[: half // 2], both[half // 2 :]], 1)
                for n in range(size * CORES // 2):
                    j, c = divmod(parity * size * CORES // 2 + n, CORES)
                    put((j, c, f), both[n * each : (n + 1) * each])

    def paired(ref, start):
        parts = [
            jnp.concatenate(
                [
                    ref[f, n, pl.ds(start, rows, stride=2)] + ref[f, n, pl.ds(start + 1, rows, stride=2)]
                    for n in range(strips)
                ],
                1,
            )
            for f in range(fields)
        ]
        return jnp.concatenate(parts, 0)

    pl.semaphore_wait(barrier, CORES * size - 1)
    for copy in rims:
        copy.start()

    for copy in fetches[: strips + 2]:
        copy.wait()

    def put_gap(at, value):
        gap[at] = -value

    def add_gap(at, value):
        gap[at] += value

    def put_mine(at, value):
        mine[at] = theirs[at] + value

    x_spectra(paired(now, 16), wide_h, wide_l, put_gap)
    for copy in fetches[strips + 2 : strips + 5]:
        copy.wait()

    @pl.when(slot == 0)
    def _():
        fresh = jnp.concatenate([incoming[f] for f in range(fields)], 0)
        x_spectra(fresh, short_h, short_l, add_gap)
        for copy in early:
            copy.start()

    @pl.when(slot == 1)
    def _():
        ahead.start()

    for copy in fetches[strips + 5 :]:
        copy.start()

    inner, edges, last = heun(wide_rows, now, first)
    inner()
    for copy in rims:
        copy.wait()
    for n in range(strips):
        across = slice(n * lanes, (n + 1) * lanes)
        now[:, n, HALO : 2 * HALO] = rim_in[0, :, :, across]
        now[:, n, 2 * HALO + wide_rows : 3 * HALO + wide_rows] = rim_in[1, :, :, across]
    edges()

    def turned(parts, sign):
        length = parts[0].shape[0]
        found = dot_split(jnp.concatenate(parts, 0), th[...], tl[...])
        cos = [found[n * length : (n + 1) * length, :half] for n in range(4)]
        sin = [found[n * length : (n + 1) * length, half:] for n in range(4)]
        return [
            (cos[n] - sign * sin[n + 1], cos[n + 1] + sign * sin[n]) for n in (0, 2)
        ]

    def y_spectra(blocks):
        low, high = blocks[: size // 2], blocks[size // 2 :]
        both = [a + b for a, b in zip(low, high)]
        apart = [a - b for a, b in zip(low, high)]
        gather = lambda pieces, at: jnp.concatenate([a[:, at * rows : (at + 1) * rows] for a in pieces], 1)
        real, imag = gather(apart, 0), gather(apart, 1)
        a, b = twiddle[0, 0:1], twiddle[1, 0:1]
        (er, ei), (our, oi) = turned(
            [gather(both, 0), gather(both, 1), real * a - imag * b, real * b + imag * a], -1.0
        )
        return jnp.concatenate([er, our, ei, oi], 1)

    def y_fields(value):
        (er, ei), (our, oi) = turned([value[:, n * half : (n + 1) * half] for n in (0, 2, 1, 3)], 1.0)
        a, b = twiddle[0, 0:1], twiddle[1, 0:1]
        our, oi = our * a + oi * b, oi * a - our * b
        blocks = []
        for real, imag in ((er + our, ei + oi), (er - our, ei - oi)):
            for n in range(size // 2):
                at = slice(n * rows, (n + 1) * rows)
                blocks.append(jnp.concatenate([real[:, at], imag[:, at]], 1))
        return blocks

    def propagate(source, target, core):
        tile = min(each, 8)
        for r in range(0, each, tile):
            at = pl.ds(core * each + r, tile)
            wave = slice(r, r + tile)
            spectra = [(source[f, wave, :nc], source[f, wave, nc:]) for f in range(fields)]
            once = apply_operator(spectra, east[at], north[:tile])
            twofold = apply_operator(once, east[at], north[:tile])
            for f in range(fields):
                for part, lanes in enumerate((slice(0, nc), slice(nc, 2 * nc))):
                    target[f, wave, lanes] = (
                        spectra[f][part] + sine[at] * once[f][part] + versine[at] * twofold[f][part]
                    )

    for copy in fetches[strips + 5 :]:
        copy.wait()

    @pl.when(slot == 1)
    def _():
        for copy in early:
            copy.wait_recv()
        order = [(c, f) for c in range(CORES) for f in range(fields)]
        value = y_spectra(
            [jnp.concatenate([landed[j, c, f] for c, f in order], 0) for j in range(size)]
        )
        for n, (c, f) in enumerate(order):
            acc[c, f] = value[n * each : (n + 1) * each]
        for c in range(CORES):
            propagate(acc.at[c], kept.at[c], c)
        relay.start()
        value = y_fields(jnp.concatenate([kept[c, f] for c, f in order], 0))
        for j in range(size):
            for n, (c, f) in enumerate(order):
                leaving[j, c, f] = value[j][n * each : (n + 1) * each]
        for copy in back:
            copy.start()

    @pl.when(slot == 0)
    def _():
        last(fine)
        for copy in early:
            copy.wait_send()
        ahead.wait_recv()
        x_spectra(paired(fine, 0), wide_h, wide_l, put_mine)
        for n in range(size):
            for c in range(CORES):
                if n > 0 or c > 0:
                    late[n][c].start()
        arrived[me] = mine[me, 0]
        relay.wait_recv()

    @pl.when(slot == 1)
    def _():
        relay.wait_send()
        relayed[...] = kept[1]
        late[0][1].wait_recv()

    for n in range(1, size):
        late[n][0].wait_recv()
    value = y_spectra([jnp.concatenate([arrived[j, f] for f in range(fields)], 0) for j in range(size)])
    for f in range(fields):
        acc[0, f] = value[f * each : (f + 1) * each] + relayed[f]

    propagate_at(propagate, acc, change, slot)
    value = y_fields(jnp.concatenate([change[f] for f in range(fields)], 0))
    for j in range(size):
        for f in range(fields):
            going[j, f] = value[j][f * each : (f + 1) * each]
    for copy in home[1:]:
        copy.start()

    @pl.when(slot == 0)
    def _():
        home[0].start()
        for n in range(size):
            for c in range(CORES):
                if n > 0 or c > 0:
                    late[n][c].wait_send()
        for copy in back:
            copy.wait_recv()

    @pl.when(slot == 1)
    def _():
        returned[me, 1] = going[me]
        last(fine)
        ahead.wait_send()
        for copy in back:
            copy.wait_send()
        homes[0][0].wait_recv()
        for n in range(1, size):
            for c in range(CORES):
                homes[n][c].wait_recv()

    turned_up, turned_down = [], []
    for f in range(fields):
        spectrum = jnp.concatenate([returned[j, c, f] for j in range(size) for c in range(CORES)], 0)
        for part, parts in zip(split(spectrum), (turned_up, turned_down)):
            wide_part = dot(mirror[...], part, (1, 1)).astype(jnp.bfloat16)
            parts.append([wide_part[:rows], wide_part[rows:]])
    sums = []
    for parity in range(2):
        at = slice(parity * half // 2, (parity + 1) * half // 2)
        up, down = (
            jnp.concatenate([jnp.concatenate([real[:, at], imag[:, at]], 1) for real, imag in parts], 0)
            for parts in (turned_up, turned_down)
        )
        both = dot(jnp.concatenate([up, down], 0), ih[parity])
        sums.append(both[: up.shape[0]] + (both[up.shape[0] :] + dot(up, il[parity])))
    stores = []
    for n in range(strips):
        at = n % (strips // 2) * lanes
        even, odd = (a[:, at : at + lanes] for a in sums)
        change_n = even + odd if n < strips // 2 else even - odd
        for f in range(fields):
            for parity in range(RATIO):
                fine[f, n, pl.ds(parity, rows, stride=RATIO)] += change_n[f * rows : (f + 1) * rows]
        stores.append(
            pltpu.make_async_copy(fine.at[:, n], out.at[:, :, pl.ds(n * lanes, lanes)], store.at[n])
        )
        stores[-1].start()

    for copy in home[1:]:
        copy.wait_send()

    @pl.when(slot == 0)
    def _():
        home[0].wait_send()

    for copy in stores:
        copy.wait()


def propagate_at(propagate, acc, change, slot):
    for core in range(CORES):
        @pl.when(slot == core)
        def _():
            propagate(acc.at[0], change, core)


def shards(start_old, incoming):
    size = lax.axis_size("space")
    state = start_old[0]
    width = state.shape[2]
    fields, rows, nc = incoming.shape
    half = nc // 2
    count = half // size
    each = count // CORES
    forward, wide, turn, twiddle, inverse, east, north, sine, versine = tables(nc)
    mirror = np.eye(2 * rows, dtype=np.float32)
    east = np.repeat(east[:, None], nc, axis=1)
    north = np.repeat(north[None, :], 8, axis=0)
    operands = [state, incoming, mirror.astype(jnp.bfloat16), north, twiddle]
    distant = [*halves(wide), *halves(forward), *halves(turn), *halves(inverse)]
    strips = width // LANES
    padded = (fields, strips, state.shape[1] + 4 * HALO, LANES)
    blocks = (size, CORES, fields, each, 2 * rows)
    single = (size, fields, each, 2 * rows)
    whole = (fields, each, 2 * nc)
    shapes = [north.shape, twiddle.shape, (2, fields, HALO, width), padded, padded]
    shapes += [(fields, strips, state.shape[1], LANES)]
    shapes += [blocks] * 4 + [single] + [(CORES, *whole)] * 2 + [whole] * 2
    shapes += [blocks, single, blocks] + [(count, nc)] * 3
    buffers = [pltpu.VMEM(incoming.shape, jnp.float32)]
    buffers += [pltpu.VMEM(mirror.shape, jnp.bfloat16)]
    buffers += [pltpu.VMEM(shape, jnp.float32) for shape in shapes]
    far = pl.BlockSpec(memory_space=pltpu.HBM)
    inputs = len(operands) + len(distant) + 3
    dma = pltpu.SemaphoreType.DMA
    result = pl.pallas_call(
        functools.partial(kernel, size),
        out_shape=jax.ShapeDtypeStruct(state.shape, jnp.float32),
        in_specs=[far] * inputs,
        out_specs=far,
        scratch_shapes=buffers
        + [pltpu.VMEM(table.shape, jnp.bfloat16) for table in distant]
        + [dma((inputs + strips,)), dma((strips,))]
        + [dma((2,))] * 4
        + [dma((size,))] * 4
        + [dma((size, CORES)), dma((size,)), dma((size,)), dma((size, CORES))],
        compiler_params=pltpu.CompilerParams(
            collective_id=0, has_side_effects=True, vmem_limit_bytes=(64 << 20) - (128 << 10)
        ),
        cost_estimate=pl.CostEstimate(
            flops=40 * fields * count * nc * nc, bytes_accessed=32 * nc * nc, transcendentals=0
        ),
    )(*operands, *distant, east, sine, versine)
    return result[None]


def solution(mesh):
    placed = (P(("group", "tm"), None, "space", None), P("group", "space", None))
    return jax.shard_map(
        shards,
        mesh=mesh,
        in_specs=placed,
        out_specs=P(("group", "tm"), None, "space", None),
        check_vma=False,
    )
```

time: 42.1 us -> 37 us (0.88)
  Pallas kernels: 39.2 us -> 34.1 us
    pallas_call x1, Pallas kernels: 39.2 us -> 34.1 us  [shards(): pl.pallas_call(functools.partial(kernel, size), out_shape=jax.ShapeDtypeS...]
where the time goes in v1:
time: 37 us; the launch traced here: 36.8 us
  Pallas kernels  34.1 us (92%)
  local copies, waits for them, and re-layouts  2.73 us (7%)
    pallas_call x1, Pallas kernels, shards(): pl.pallas_call(functools.partial(kernel, size), out_shape=jax.ShapeDtypeS...  34.1 us
    unnamed x1, local copies, waits for them, and re-layouts  2.73 us

profile of v1, /device:TPU:1, one launch (start us, length us, event | category | flops | bytes accessed | tf_op | source)
XLA Modules:
  0.0 36.8 jit_solution(5275304561106499208)
XLA Ops:
  0.0 34.1 %shard_map.154 = f32[3,128,1024]{2,1,0:T(8,128)} custom-call(f32[3,128,1024]{2,1,0:T(8,128)} %bitcast.3, f32[3,64,512]{2,1,0:T(8,128)} %incoming_far.1, bf16[128,128]{1,0:T(8,128)(2,1)} %constant.28.clone.mirror_far, f32[8,512]{1,0:T(8,128)} %constant.29.clone.north_far, f32[2,8,256]{2,1,0:T(8,128)} %constant.30.clone.twiddle_far, ...), custom_call_target="tpu_custom_call" | custom-call | flops 1006632960 | bytes 8388608 | tf_op jit(solution)/shard_map/pallas_call | solution.py:538
  34.1 2.7 %copy.18 = f32[1,3,128,1024]{3,2,1,0:T(8,128)} copy(f32[1,3,128,1024]{3,2,1,0:T(8,128)} %bitcast.2) | data formatting | bytes 3145728

commit v2 on v1

--- a/solution.py
+++ b/solution.py
@@ -120,48 +120,56 @@
         yield n, (h, u, v), (rate_h, rate_u, rate_v)
 
 
-def heun(rows, now, first):
+def loop(start, stop, body):
+    count = stop - start
+    if count > 0:
+        unroll = max(n for n in range(1, 9) if count % n == 0)
+        lax.fori_loop(start, stop, lambda n, _: body(n), None, unroll=unroll)
+
+
+def heun(rows, now, first, fine):
     blocks = (rows + 2 * HALO) // 8
     unit = 0.5 * TIME_STEP
 
     def rows_at(block):
-        return block * 8 if isinstance(block, int) else pl.multiple_of(block * 8, 8)
-
-    def predict(block, _):
+        return pl.multiple_of(block * 8, 8)
+
+    def predict(block):
         at = rows_at(block + 1)
-        for n, mid, rate in slopes(now, at):
-            for f in range(3):
-                first[f, n, pl.ds(at, 8)] = mid[f] - unit * rate[f]
-        return 0
+        found = [(f, n, mid[f] - unit * rate[f]) for n, mid, rate in slopes(now, at) for f in range(3)]
+        for f, n, value in found:
+            first[f, n, pl.ds(at, 8)] = value
 
     def correct(out, shift):
-        def body(block, _):
+        def body(block):
             at, to = rows_at(block + 1), rows_at(block + 1 - shift)
-            for n, mid, rate in slopes(first, at):
-                for f in range(3):
-                    out[f, n, pl.ds(to, 8)] = (
-                        0.5 * (now[f, n, pl.ds(at, 8)] + mid[f]) - (0.5 * unit) * rate[f]
-                    )
-            return 0
+            found = [
+                (f, n, 0.5 * (now[f, n, pl.ds(at, 8)] + mid[f]) - (0.5 * unit) * rate[f])
+                for n, mid, rate in slopes(first, at)
+                for f in range(3)
+            ]
+            for f, n, value in found:
+                out[f, n, pl.ds(to, 8)] = value
 
         return body
 
-    def inner():
-        lax.fori_loop(2, blocks - 2, predict, 0)
-
-    def edges():
-        def edge(n, _):
-            predict(jnp.where(n < 2, n, n + blocks - 4), 0)
-            return 0
-
-        lax.fori_loop(0, 4, edge, 0)
-        lax.fori_loop(0, blocks, correct(now, 0), 0)
-
-    def last(fine):
-        lax.fori_loop(0, blocks, predict, 0)
-        lax.fori_loop(1, blocks - 1, correct(fine, 2), 0)
-
-    return inner, edges, last
+    stages = [(predict, 0), (correct(now, 0), 0), (predict, 0), (correct(fine, 2), 1)]
+
+    def inside():
+        for depth, (body, _) in enumerate(stages):
+            loop(2 + depth, blocks - 2 - depth, body)
+
+    def outside():
+        for depth, (body, begin) in enumerate(stages):
+            low, high = 2 + depth, blocks - 2 - depth
+            if low < high:
+                side = low - begin
+                skip = high - low
+                loop(0, 2 * side, lambda n: body(jnp.where(n < side, n, n + skip) + begin))
+            else:
+                loop(begin, blocks - begin, body)
+
+    return inside, outside
 
 
 def apply_operator(s, a, b):
@@ -291,30 +299,33 @@
         ]
         return jnp.concatenate(parts, 0)
 
+    for copy in fetches[: strips + 2]:
+        copy.wait()
+
+    def put_gap(at, value):
+        gap[at] = -value
+
+    def add_gap(at, value):
+        gap[at] += value
+
+    def put_mine(at, value):
+        mine[at] = theirs[at] + value
+
+    x_spectra(paired(now, 16), wide_h, wide_l, put_gap)
+    for copy in fetches[strips + 2 : strips + 5]:
+        copy.wait()
+
+    @pl.when(slot == 0)
+    def _():
+        fresh = jnp.concatenate([incoming[f] for f in range(fields)], 0)
+        x_spectra(fresh, short_h, short_l, add_gap)
+
     pl.semaphore_wait(barrier, CORES * size - 1)
     for copy in rims:
         copy.start()
 
-    for copy in fetches[: strips + 2]:
-        copy.wait()
-
-    def put_gap(at, value):
-        gap[at] = -value
-
-    def add_gap(at, value):
-        gap[at] += value
-
-    def put_mine(at, value):
-        mine[at] = theirs[at] + value
-
-    x_spectra(paired(now, 16), wide_h, wide_l, put_gap)
-    for copy in fetches[strips + 2 : strips + 5]:
-        copy.wait()
-
     @pl.when(slot == 0)
     def _():
-        fresh = jnp.concatenate([incoming[f] for f in range(fields)], 0)
-        x_spectra(fresh, short_h, short_l, add_gap)
         for copy in early:
             copy.start()
 
@@ -325,15 +336,15 @@
     for copy in fetches[strips + 5 :]:
         copy.start()
 
-    inner, edges, last = heun(wide_rows, now, first)
-    inner()
+    inside, outside = heun(wide_rows, now, first, fine)
+    inside()
     for copy in rims:
         copy.wait()
     for n in range(strips):
         across = slice(n * lanes, (n + 1) * lanes)
         now[:, n, HALO : 2 * HALO] = rim_in[0, :, :, across]
         now[:, n, 2 * HALO + wide_rows : 3 * HALO + wide_rows] = rim_in[1, :, :, across]
-    edges()
+    outside()
 
     def turned(parts, sign):
         length = parts[0].shape[0]
@@ -406,7 +417,6 @@
 
     @pl.when(slot == 0)
     def _():
-        last(fine)
         for copy in early:
             copy.wait_send()
         ahead.wait_recv()
@@ -451,7 +461,6 @@
     @pl.when(slot == 1)
     def _():
         returned[me, 1] = going[me]
-        last(fine)
         ahead.wait_send()
         for copy in back:
             copy.wait_send()

time: 37 us -> 34.8 us (0.941)
  Pallas kernels: 34.1 us -> 32 us
    pallas_call x1, Pallas kernels: 34.1 us -> 32 us  [shards(): pl.pallas_call(functools.partial(kernel, size), out_shape=jax.ShapeDtypeS...]
where the time goes in v2:
time: 34.8 us; the launch traced here: 34.7 us
  Pallas kernels  32 us (92%)
  local copies, waits for them, and re-layouts  2.73 us (8%)
    pallas_call x1, Pallas kernels, shards(): pl.pallas_call(functools.partial(kernel, size), out_shape=jax.ShapeDtypeS...  32 us
    unnamed x1, local copies, waits for them, and re-layouts  2.73 us

profile of v2, /device:TPU:1, one launch (start us, length us, event | category | flops | bytes accessed | tf_op | source)
XLA Modules:
  0.0 34.7 jit_solution(17649146969384090498)
XLA Ops:
  0.0 32.0 %shard_map.154 = f32[3,128,1024]{2,1,0:T(8,128)} custom-call(f32[3,128,1024]{2,1,0:T(8,128)} %bitcast.3, f32[3,64,512]{2,1,0:T(8,128)} %incoming_far.1, bf16[128,128]{1,0:T(8,128)(2,1)} %constant.28.clone.mirror_far, f32[8,512]{1,0:T(8,128)} %constant.29.clone.north_far, f32[2,8,256]{2,1,0:T(8,128)} %constant.30.clone.twiddle_far, ...), custom_call_target="tpu_custom_call" | custom-call | flops 1006632960 | bytes 8388608 | tf_op jit(solution)/shard_map/pallas_call | solution.py:547
  32.0 2.7 %copy.18 = f32[1,3,128,1024]{3,2,1,0:T(8,128)} copy(f32[1,3,128,1024]{3,2,1,0:T(8,128)} %bitcast.2) | data formatting | bytes 3145728

commit v3 on v2

--- a/solution.py
+++ b/solution.py
@@ -184,11 +184,11 @@
 def kernel(
     size, state, incoming_far, mirror_far, north_far, twiddle_far,
     wide_h_far, wide_l_far, short_h_far, short_l_far, turn_h, turn_l, inverse_h, inverse_l,
-    east_far, sine_far, versine_far, out,
-    incoming, mirror, north, twiddle, rim_in, now, first, fine, gap, mine, theirs, landed, arrived, acc, kept, relayed, change,
+    east_far, sine_far, versine_far, fine,
+    incoming, mirror, north, twiddle, rim_in, now, first, gap, mine, theirs, landed, arrived, acc, kept, relayed, change,
     leaving, going, returned, east, sine, versine,
     wide_h, wide_l, short_h, short_l, th, tl, ih, il,
-    fetch, store, rim_send, rim_recv, t_send, t_recv, d_send, d_recv, e_send, e_recv, g_send, g_recv, h_send, h_recv,
+    fetch, rim_send, rim_recv, t_send, t_recv, d_send, d_recv, e_send, e_recv, g_send, g_recv, h_send, h_recv,
 ):
     fields, rows, nc = incoming_far.shape
     wide_rows, width = state.shape[1:]
@@ -484,7 +484,6 @@
         )
         both = dot(jnp.concatenate([up, down], 0), ih[parity])
         sums.append(both[: up.shape[0]] + (both[up.shape[0] :] + dot(up, il[parity])))
-    stores = []
     for n in range(strips):
         at = n % (strips // 2) * lanes
         even, odd = (a[:, at : at + lanes] for a in sums)
@@ -492,10 +491,6 @@
         for f in range(fields):
             for parity in range(RATIO):
                 fine[f, n, pl.ds(parity, rows, stride=RATIO)] += change_n[f * rows : (f + 1) * rows]
-        stores.append(
-            pltpu.make_async_copy(fine.at[:, n], out.at[:, :, pl.ds(n * lanes, lanes)], store.at[n])
-        )
-        stores[-1].start()
 
     for copy in home[1:]:
         copy.wait_send()
@@ -504,7 +499,16 @@
     def _():
         home[0].wait_send()
 
-    for copy in stores:
+
+def hand_over(fine, out, sem):
+    strips, lanes = fine.shape[1], fine.shape[3]
+    copies = [
+        pltpu.make_async_copy(fine.at[:, n], out.at[:, :, pl.ds(n * lanes, lanes)], sem.at[n])
+        for n in range(strips)
+    ]
+    for copy in copies:
+        copy.start()
+    for copy in copies:
         copy.wait()
 
 
@@ -535,7 +539,6 @@
     single = (size, fields, each, 2 * rows)
     whole = (fields, each, 2 * nc)
     shapes = [north.shape, twiddle.shape, (2, fields, HALO, width), padded, padded]
-    shapes += [(fields, strips, state.shape[1], LANES)]
     shapes += [blocks] * 4 + [single] + [(CORES, *whole)] * 2 + [whole] * 2
     shapes += [blocks, single, blocks] + [(count, nc)] * 3
     buffers = [pltpu.VMEM(incoming.shape, jnp.float32)]
@@ -546,22 +549,30 @@
     dma = pltpu.SemaphoreType.DMA
     result = pl.pallas_call(
         functools.partial(kernel, size),
-        out_shape=jax.ShapeDtypeStruct(state.shape, jnp.float32),
+        out_shape=pltpu.VMEM((fields, strips, state.shape[1], LANES), jnp.float32),
         in_specs=[far] * inputs,
-        out_specs=far,
+        out_specs=pl.BlockSpec(memory_space=pltpu.VMEM),
         scratch_shapes=buffers
         + [pltpu.VMEM(table.shape, jnp.bfloat16) for table in distant]
-        + [dma((inputs + strips,)), dma((strips,))]
+        + [dma((inputs + strips,))]
         + [dma((2,))] * 4
         + [dma((size,))] * 4
         + [dma((size, CORES)), dma((size,)), dma((size,)), dma((size, CORES))],
         compiler_params=pltpu.CompilerParams(
-            collective_id=0, has_side_effects=True, vmem_limit_bytes=(64 << 20) - (128 << 10)
+            collective_id=0, has_side_effects=True, vmem_limit_bytes=48 << 20
         ),
         cost_estimate=pl.CostEstimate(
             flops=40 * fields * count * nc * nc, bytes_accessed=32 * nc * nc, transcendentals=0
         ),
-    )(*operands, *distant, east, sine, versine)
+    )(*(pltpu.with_memory_space_constraint(a, pltpu.HBM) for a in (*operands, *distant, east, sine, versine)))
+    result = pl.pallas_call(
+        hand_over,
+        out_shape=jax.ShapeDtypeStruct(state.shape, jnp.float32),
+        in_specs=[pl.BlockSpec(memory_space=pltpu.VMEM)],
+        out_specs=far,
+        scratch_shapes=[dma((strips,))],
+        compiler_params=pltpu.CompilerParams(vmem_limit_bytes=16 << 20),
+    )(pltpu.with_memory_space_constraint(result, pltpu.VMEM))
     return result[None]
 
 

time: 34.8 us -> 32.2 us (0.925)
  local copies, waits for them, and re-layouts: 2.73 us -> 0 us
    unnamed x1 -> x0, local copies, waits for them, and re-layouts: 2.73 us -> none
    pallas_call x1 -> x2, Pallas kernels: 32 us -> 32 us  [the longest x1 30.8 us: shards(): pl.pallas_call(functools.partial(kernel, size), out_shape=pltpu.VMEM((fie...]
where the time goes in v3:
time: 32.2 us; the launch traced here: 32 us
  Pallas kernels  32 us (99%)
    pallas_call x1, Pallas kernels, shards(): pl.pallas_call(functools.partial(kernel, size), out_shape=pltpu.VMEM((fie...  30.8 us
    pallas_call x1, Pallas kernels, shards(): pl.pallas_call(hand_over, out_shape=jax.ShapeDtypeStruct(state.shape, jnp...  1.2 us

profile of v3, /device:TPU:1, one launch (start us, length us, event | category | flops | bytes accessed | tf_op | source)
XLA Modules:
  0.0 32.0 jit_solution(7781109867749595753)
XLA Ops:
  0.0 30.8 %shard_map.154.fine = f32[3,8,128,128]{3,2,1,0:T(8,128)S(1)} custom-call(f32[3,128,1024]{2,1,0:T(8,128)} %bitcast.2, f32[3,64,512]{2,1,0:T(8,128)} %incoming_far.1, bf16[128,128]{1,0:T(8,128)(2,1)} %constant.28.clone.mirror_far, f32[8,512]{1,0:T(8,128)} %constant.29.clone.north_far, f32[2,8,256]{2,1,0:T(8,128)} %constant.30.clone.twiddle_far, ...), custom_call_target="tpu_custom_call" | custom-call | flops 1006632960 | bytes 8388608 | tf_op jit(solution)/shard_map/pallas_call | solution.py:550
  30.8 1.2 %shard_map.155 = f32[3,128,1024]{2,1,0:T(8,128)} custom-call(f32[3,8,128,128]{3,2,1,0:T(8,128)S(1)} %shard_map.154.fine), custom_call_target="tpu_custom_call" | custom-call | tf_op jit(solution)/shard_map/pallas_call | solution.py:568

commit v4 on v3

--- a/solution.py
+++ b/solution.py
@@ -312,20 +312,17 @@
         mine[at] = theirs[at] + value
 
     x_spectra(paired(now, 16), wide_h, wide_l, put_gap)
-    for copy in fetches[strips + 2 : strips + 5]:
-        copy.wait()
-
-    @pl.when(slot == 0)
-    def _():
-        fresh = jnp.concatenate([incoming[f] for f in range(fields)], 0)
-        x_spectra(fresh, short_h, short_l, add_gap)
-
     pl.semaphore_wait(barrier, CORES * size - 1)
     for copy in rims:
         copy.start()
 
+    for copy in fetches[strips + 2 : strips + 5]:
+        copy.wait()
+
     @pl.when(slot == 0)
     def _():
+        fresh = jnp.concatenate([incoming[f] for f in range(fields)], 0)
+        x_spectra(fresh, short_h, short_l, add_gap)
         for copy in early:
             copy.start()
 
@@ -417,8 +414,6 @@
 
     @pl.when(slot == 0)
     def _():
-        for copy in early:
-            copy.wait_send()
         ahead.wait_recv()
         x_spectra(paired(fine, 0), wide_h, wide_l, put_mine)
         for n in range(size):
@@ -455,6 +450,8 @@
             for c in range(CORES):
                 if n > 0 or c > 0:
                     late[n][c].wait_send()
+        for copy in early:
+            copy.wait_send()
         for copy in back:
             copy.wait_recv()
 

time: 32.2 us -> 31.2 us (0.969)
  Pallas kernels: 32 us -> 31 us
    pallas_call x1, Pallas kernels: 30.8 us -> 29.8 us  [shards(): pl.pallas_call(functools.partial(kernel, size), out_shape=pltpu.VMEM((fie...]
where the time goes in v4:
time: 31.2 us; the launch traced here: 31 us
  Pallas kernels  31 us (99%)
    pallas_call x1, Pallas kernels, shards(): pl.pallas_call(functools.partial(kernel, size), out_shape=pltpu.VMEM((fie...  29.8 us
    pallas_call x1, Pallas kernels, shards(): pl.pallas_call(hand_over, out_shape=jax.ShapeDtypeStruct(state.shape, jnp...  1.2 us

profile of v4, /device:TPU:1, one launch (start us, length us, event | category | flops | bytes accessed | tf_op | source)
XLA Modules:
  0.0 31.0 jit_solution(5815299706696576938)
XLA Ops:
  0.0 29.8 %shard_map.154.fine = f32[3,8,128,128]{3,2,1,0:T(8,128)S(1)} custom-call(f32[3,128,1024]{2,1,0:T(8,128)} %bitcast.2, f32[3,64,512]{2,1,0:T(8,128)} %incoming_far.1, bf16[128,128]{1,0:T(8,128)(2,1)} %constant.28.clone.mirror_far, f32[8,512]{1,0:T(8,128)} %constant.29.clone.north_far, f32[2,8,256]{2,1,0:T(8,128)} %constant.30.clone.twiddle_far, ...), custom_call_target="tpu_custom_call" | custom-call | flops 1006632960 | bytes 8388608 | tf_op jit(solution)/shard_map/pallas_call | solution.py:547
  29.8 1.2 %shard_map.155 = f32[3,128,1024]{2,1,0:T(8,128)} custom-call(f32[3,8,128,128]{3,2,1,0:T(8,128)S(1)} %shard_map.154.fine), custom_call_target="tpu_custom_call" | custom-call | tf_op jit(solution)/shard_map/pallas_call | solution.py:565

commit v5 on v4

--- a/solution.py
+++ b/solution.py
@@ -184,8 +184,8 @@
 def kernel(
     size, state, incoming_far, mirror_far, north_far, twiddle_far,
     wide_h_far, wide_l_far, short_h_far, short_l_far, turn_h, turn_l, inverse_h, inverse_l,
-    east_far, sine_far, versine_far, fine,
-    incoming, mirror, north, twiddle, rim_in, now, first, gap, mine, theirs, landed, arrived, acc, kept, relayed, change,
+    east_far, sine_far, versine_far, fine, sums,
+    incoming, mirror, north, twiddle, rim_in, now, first, gap, mine, theirs, landed, arrived, acc, kept, change,
     leaving, going, returned, east, sine, versine,
     wide_h, wide_l, short_h, short_l, th, tl, ih, il,
     fetch, rim_send, rim_recv, t_send, t_recv, d_send, d_recv, e_send, e_recv, g_send, g_recv, h_send, h_recv,
@@ -195,7 +195,7 @@
     strips, lanes = now.shape[1], now.shape[3]
     half = nc // 2
     count = half // size
-    each = count // CORES
+    each = count // 2
     me, slot = lax.axis_index("space"), lax.axis_index("tm")
     peers = [lax.rem(me + d, size) for d in range(size)]
     origins = [lax.rem(me + size - d, size) for d in range(size)]
@@ -259,22 +259,17 @@
     ]
     early = [send(gap.at[p], landed.at[me], d_send.at[n], d_recv.at[n], p, 1) for n, p in enumerate(peers)]
     ahead = send(gap, theirs, t_send.at[0], t_recv.at[0], me, 0)
-    relay = send(kept.at[0], relayed, t_send.at[1], t_recv.at[1], me, 0)
     back = [send(leaving.at[p], returned.at[me], e_send.at[n], e_recv.at[n], p, 0) for n, p in enumerate(peers)]
     late = [
-        [send(mine.at[p, c], arrived.at[me], g_send.at[n, c], g_recv.at[n], p, c) for c in range(CORES)]
+        [send(mine.at[p, h], arrived.at[me, h], g_send.at[n, h], g_recv.at[n, h], p, 1) for h in range(2)]
         for n, p in enumerate(peers)
     ]
     home = [
-        send(going.at[p], returned.at[me, slot], h_send.at[n], h_recv.at[n, slot], p, 1)
+        [send(going.at[p, h], returned.at[me, h], h_send.at[n, h], h_recv.at[n, h], p, 1) for h in range(2)]
         for n, p in enumerate(peers)
     ]
-    homes = [
-        [send(going.at[p], returned.at[me, c], h_send.at[n], h_recv.at[n, c], p, 1) for c in range(CORES)]
-        for n, p in enumerate(peers)
-    ]
-
-    def x_spectra(value, high, low, put):
+
+    def x_spectra(value, high, low, put, done=None):
         middle = value.shape[1] // 2
         west, east_side = value[:, :middle], value[:, middle:]
         for parity, part in enumerate((west + east_side, west - east_side)):
@@ -282,9 +277,10 @@
             for f in range(fields):
                 both = found[:, f * rows : (f + 1) * rows]
                 both = jnp.concatenate([both[: half // 2], both[half // 2 :]], 1)
-                for n in range(size * CORES // 2):
-                    j, c = divmod(parity * size * CORES // 2 + n, CORES)
-                    put((j, c, f), both[n * each : (n + 1) * each])
+                for n in range(size):
+                    put((n, parity, f), both[n * each : (n + 1) * each])
+            if done is not None:
+                done(parity)
 
     def paired(ref, start):
         parts = [
@@ -375,10 +371,10 @@
                 blocks.append(jnp.concatenate([real[:, at], imag[:, at]], 1))
         return blocks
 
-    def propagate(source, target, core):
+    def propagate(source, target, parity):
         tile = min(each, 8)
         for r in range(0, each, tile):
-            at = pl.ds(core * each + r, tile)
+            at = pl.ds(parity * each + r, tile)
             wave = slice(r, r + tile)
             spectra = [(source[f, wave, :nc], source[f, wave, nc:]) for f in range(fields)]
             once = apply_operator(spectra, east[at], north[:tile])
@@ -396,60 +392,31 @@
     def _():
         for copy in early:
             copy.wait_recv()
-        order = [(c, f) for c in range(CORES) for f in range(fields)]
-        value = y_spectra(
-            [jnp.concatenate([landed[j, c, f] for c, f in order], 0) for j in range(size)]
-        )
-        for n, (c, f) in enumerate(order):
-            acc[c, f] = value[n * each : (n + 1) * each]
-        for c in range(CORES):
-            propagate(acc.at[c], kept.at[c], c)
-        relay.start()
-        value = y_fields(jnp.concatenate([kept[c, f] for c, f in order], 0))
+        order = [(h, f) for h in range(2) for f in range(fields)]
+        value = y_spectra([jnp.concatenate([landed[j, h, f] for h, f in order], 0) for j in range(size)])
+        for n, (h, f) in enumerate(order):
+            acc[h, f] = value[n * each : (n + 1) * each]
+        for h in range(2):
+            propagate(acc.at[h], kept.at[h], h)
+        value = y_fields(jnp.concatenate([kept[h, f] for h, f in order], 0))
         for j in range(size):
-            for n, (c, f) in enumerate(order):
-                leaving[j, c, f] = value[j][n * each : (n + 1) * each]
+            for n, (h, f) in enumerate(order):
+                leaving[j, h, f] = value[j][n * each : (n + 1) * each]
         for copy in back:
             copy.start()
 
     @pl.when(slot == 0)
     def _():
         ahead.wait_recv()
-        x_spectra(paired(fine, 0), wide_h, wide_l, put_mine)
-        for n in range(size):
-            for c in range(CORES):
-                if n > 0 or c > 0:
-                    late[n][c].start()
-        arrived[me] = mine[me, 0]
-        relay.wait_recv()
-
-    @pl.when(slot == 1)
-    def _():
-        relay.wait_send()
-        relayed[...] = kept[1]
-        late[0][1].wait_recv()
-
-    for n in range(1, size):
-        late[n][0].wait_recv()
-    value = y_spectra([jnp.concatenate([arrived[j, f] for f in range(fields)], 0) for j in range(size)])
-    for f in range(fields):
-        acc[0, f] = value[f * each : (f + 1) * each] + relayed[f]
-
-    propagate_at(propagate, acc, change, slot)
-    value = y_fields(jnp.concatenate([change[f] for f in range(fields)], 0))
-    for j in range(size):
-        for f in range(fields):
-            going[j, f] = value[j][f * each : (f + 1) * each]
-    for copy in home[1:]:
-        copy.start()
-
-    @pl.when(slot == 0)
-    def _():
-        home[0].start()
-        for n in range(size):
-            for c in range(CORES):
-                if n > 0 or c > 0:
-                    late[n][c].wait_send()
+
+        def depart(h):
+            for copies in late:
+                copies[h].start()
+
+        x_spectra(paired(fine, 0), wide_h, wide_l, put_mine, depart)
+        for copies in late:
+            for copy in copies:
+                copy.wait_send()
         for copy in early:
             copy.wait_send()
         for copy in back:
@@ -457,63 +424,67 @@
 
     @pl.when(slot == 1)
     def _():
-        returned[me, 1] = going[me]
+        for h in range(2):
+            for copies in late:
+                copies[h].wait_recv()
+            value = y_spectra(
+                [jnp.concatenate([arrived[j, h, f] for f in range(fields)], 0) for j in range(size)]
+            )
+            for f in range(fields):
+                acc[h, f] = value[f * each : (f + 1) * each] + kept[h, f]
+            propagate(acc.at[h], change.at[h], h)
+            value = y_fields(jnp.concatenate([change[h, f] for f in range(fields)], 0))
+            for j in range(size):
+                for f in range(fields):
+                    going[j, h, f] = value[j][f * each : (f + 1) * each]
+            for copies in home[1:]:
+                copies[h].start()
+            returned[me, h] = going[me, h]
         ahead.wait_send()
         for copy in back:
             copy.wait_send()
-        homes[0][0].wait_recv()
-        for n in range(1, size):
-            for c in range(CORES):
-                homes[n][c].wait_recv()
-
-    turned_up, turned_down = [], []
-    for f in range(fields):
-        spectrum = jnp.concatenate([returned[j, c, f] for j in range(size) for c in range(CORES)], 0)
-        for part, parts in zip(split(spectrum), (turned_up, turned_down)):
-            wide_part = dot(mirror[...], part, (1, 1)).astype(jnp.bfloat16)
-            parts.append([wide_part[:rows], wide_part[rows:]])
-    sums = []
-    for parity in range(2):
-        at = slice(parity * half // 2, (parity + 1) * half // 2)
-        up, down = (
-            jnp.concatenate([jnp.concatenate([real[:, at], imag[:, at]], 1) for real, imag in parts], 0)
-            for parts in (turned_up, turned_down)
-        )
-        both = dot(jnp.concatenate([up, down], 0), ih[parity])
-        sums.append(both[: up.shape[0]] + (both[up.shape[0] :] + dot(up, il[parity])))
+
+    for h in range(2):
+        @pl.when(slot == 1)
+        def _():
+            for copies in home[1:]:
+                copies[h].wait_recv()
+
+        turned_up, turned_down = [], []
+        for f in range(fields):
+            spectrum = jnp.concatenate([returned[j, h, f] for j in range(size)], 0)
+            for part, parts in zip(split(spectrum), (turned_up, turned_down)):
+                flipped = dot(mirror[...], part, (1, 1)).astype(jnp.bfloat16)
+                parts.append(jnp.concatenate([flipped[:rows], flipped[rows:]], 1))
+        up, down = jnp.concatenate(turned_up, 0), jnp.concatenate(turned_down, 0)
+        both = dot(jnp.concatenate([up, down], 0), ih[h])
+        total = both[: up.shape[0]] + (both[up.shape[0] :] + dot(up, il[h]))
+        sums[h] = total
+    @pl.when(slot == 1)
+    def _():
+        for copies in home[1:]:
+            for copy in copies:
+                copy.wait_send()
+
+
+def finish(fine, sums, out, held, sem):
+    fields, strips, wide_rows, lanes = fine.shape
+    rows = wide_rows // RATIO
+    copies = []
     for n in range(strips):
         at = n % (strips // 2) * lanes
-        even, odd = (a[:, at : at + lanes] for a in sums)
-        change_n = even + odd if n < strips // 2 else even - odd
+        even, odd = (sums[h, :, at : at + lanes] for h in range(2))
+        change = even + odd if n < strips // 2 else even - odd
         for f in range(fields):
             for parity in range(RATIO):
-                fine[f, n, pl.ds(parity, rows, stride=RATIO)] += change_n[f * rows : (f + 1) * rows]
-
-    for copy in home[1:]:
-        copy.wait_send()
-
-    @pl.when(slot == 0)
-    def _():
-        home[0].wait_send()
-
-
-def hand_over(fine, out, sem):
-    strips, lanes = fine.shape[1], fine.shape[3]
-    copies = [
-        pltpu.make_async_copy(fine.at[:, n], out.at[:, :, pl.ds(n * lanes, lanes)], sem.at[n])
-        for n in range(strips)
-    ]
-    for copy in copies:
-        copy.start()
+                at = pl.ds(parity, rows, stride=RATIO)
+                held[f, n, at] = fine[f, n, at] + change[f * rows : (f + 1) * rows]
+        copies.append(
+            pltpu.make_async_copy(held.at[:, n], out.at[:, :, pl.ds(n * lanes, lanes)], sem.at[n])
+        )
+        copies[-1].start()
     for copy in copies:
         copy.wait()
-
-
-def propagate_at(propagate, acc, change, slot):
-    for core in range(CORES):
-        @pl.when(slot == core)
-        def _():
-            propagate(acc.at[0], change, core)
 
 
 def shards(start_old, incoming):
@@ -523,38 +494,42 @@
     fields, rows, nc = incoming.shape
     half = nc // 2
     count = half // size
-    each = count // CORES
+    each = count // 2
     forward, wide, turn, twiddle, inverse, east, north, sine, versine = tables(nc)
     mirror = np.eye(2 * rows, dtype=np.float32)
-    east = np.repeat(east[:, None], nc, axis=1)
+    chipwise = lambda a: a.reshape(2, size, each, -1).transpose(1, 0, 2, 3).reshape(half, -1)
+    east, sine, versine = chipwise(np.repeat(east[:, None], nc, axis=1)), chipwise(sine), chipwise(versine)
     north = np.repeat(north[None, :], 8, axis=0)
     operands = [state, incoming, mirror.astype(jnp.bfloat16), north, twiddle]
     distant = [*halves(wide), *halves(forward), *halves(turn), *halves(inverse)]
     strips = width // LANES
     padded = (fields, strips, state.shape[1] + 4 * HALO, LANES)
-    blocks = (size, CORES, fields, each, 2 * rows)
-    single = (size, fields, each, 2 * rows)
-    whole = (fields, each, 2 * nc)
+    blocks = (size, 2, fields, each, 2 * rows)
+    whole = (2, fields, each, 2 * nc)
     shapes = [north.shape, twiddle.shape, (2, fields, HALO, width), padded, padded]
-    shapes += [blocks] * 4 + [single] + [(CORES, *whole)] * 2 + [whole] * 2
-    shapes += [blocks, single, blocks] + [(count, nc)] * 3
+    shapes += [blocks] * 5 + [whole] * 3
+    shapes += [blocks] * 3 + [(count, nc)] * 3
     buffers = [pltpu.VMEM(incoming.shape, jnp.float32)]
     buffers += [pltpu.VMEM(mirror.shape, jnp.bfloat16)]
     buffers += [pltpu.VMEM(shape, jnp.float32) for shape in shapes]
     far = pl.BlockSpec(memory_space=pltpu.HBM)
     inputs = len(operands) + len(distant) + 3
     dma = pltpu.SemaphoreType.DMA
-    result = pl.pallas_call(
+    found = pl.pallas_call(
         functools.partial(kernel, size),
-        out_shape=pltpu.VMEM((fields, strips, state.shape[1], LANES), jnp.float32),
+        out_shape=[
+            pltpu.VMEM((fields, strips, state.shape[1], LANES), jnp.float32),
+            pltpu.VMEM((2, fields * rows, width // 2), jnp.float32),
+        ],
         in_specs=[far] * inputs,
-        out_specs=pl.BlockSpec(memory_space=pltpu.VMEM),
+        out_specs=[pl.BlockSpec(memory_space=pltpu.VMEM)] * 2,
         scratch_shapes=buffers
         + [pltpu.VMEM(table.shape, jnp.bfloat16) for table in distant]
         + [dma((inputs + strips,))]
-        + [dma((2,))] * 4
+        + [dma((2,))] * 2
+        + [dma((1,))] * 2
         + [dma((size,))] * 4
-        + [dma((size, CORES)), dma((size,)), dma((size,)), dma((size, CORES))],
+        + [dma((size, 2))] * 4,
         compiler_params=pltpu.CompilerParams(
             collective_id=0, has_side_effects=True, vmem_limit_bytes=48 << 20
         ),
@@ -563,13 +538,13 @@
         ),
     )(*(pltpu.with_memory_space_constraint(a, pltpu.HBM) for a in (*operands, *distant, east, sine, versine)))
     result = pl.pallas_call(
-        hand_over,
+        finish,
         out_shape=jax.ShapeDtypeStruct(state.shape, jnp.float32),
-        in_specs=[pl.BlockSpec(memory_space=pltpu.VMEM)],
+        in_specs=[pl.BlockSpec(memory_space=pltpu.VMEM)] * 2,
         out_specs=far,
-        scratch_shapes=[dma((strips,))],
+        scratch_shapes=[pltpu.VMEM(found[0].shape, jnp.float32), dma((strips,))],
         compiler_params=pltpu.CompilerParams(vmem_limit_bytes=16 << 20),
-    )(pltpu.with_memory_space_constraint(result, pltpu.VMEM))
+    )(*(pltpu.with_memory_space_constraint(a, pltpu.VMEM) for a in found))
     return result[None]
 
 

time: 31.2 us -> 30 us (0.962)
  Pallas kernels: 31 us -> 29.8 us
    pallas_call x2, Pallas kernels: 31 us -> 29.8 us  [the longest x1 28.6 us: shards(): pl.pallas_call(functools.partial(kernel, size), out_shape=[pltpu.VMEM((fi...]
where the time goes in v5:
time: 30 us; the launch traced here: 29.8 us
  Pallas kernels  29.8 us (99%)
    pallas_call x1, Pallas kernels, shards(): pl.pallas_call(functools.partial(kernel, size), out_shape=[pltpu.VMEM((fi...  28.6 us
    pallas_call x1, Pallas kernels, shards(): pl.pallas_call(finish, out_shape=jax.ShapeDtypeStruct(state.shape, jnp.fl...  1.23 us

profile of v5, /device:TPU:1, one launch (start us, length us, event | category | flops | bytes accessed | tf_op | source)
XLA Modules:
  0.0 29.8 jit_solution(17681466951054121900)
XLA Ops:
  0.0 28.6 %shard_map.154 = (f32[3,8,128,128]{3,2,1,0:T(8,128)S(1)}, f32[2,192,512]{2,1,0:T(8,128)S(1)}) custom-call(f32[3,128,1024]{2,1,0:T(8,128)} %bitcast.2, f32[3,64,512]{2,1,0:T(8,128)} %incoming_far.1, bf16[128,128]{1,0:T(8,128)(2,1)} %constant.28.clone.mirror_far, f32[8,512]{1,0:T(8,128)} %constant.29.clone.north_far, f32[2,8,256]{2,1,0:T(8,128)} %constant.30.clone.twiddle_far, ...), custom_call_target="tpu_custom_call" | custom-call | flops 1006632960 | bytes 8388608 | tf_op jit(solution)/shard_map/pallas_call | solution.py:518
  28.6 1.2 %shard_map.155 = f32[3,128,1024]{2,1,0:T(8,128)} custom-call(f32[3,8,128,128]{3,2,1,0:T(8,128)S(1)} %get-tuple-element.7.fine, f32[2,192,512]{2,1,0:T(8,128)S(1)} %get-tuple-element.8.sums), custom_call_target="tpu_custom_call" | custom-call | tf_op jit(solution)/shard_map/pallas_call | solution.py:540
